TPU v7x, 32 devices: a whole 2x2x4 slice. The times are simulated.
32 devices in a mesh: leaf: 8 (over z, y), rhs: 4 (over x, core).
Axes of the slice: x: 2, y: 2, z: 4, core: 2. Of those that a mesh axis runs over, the one named last changes fastest.
Arguments:
- obs_coef: float32 [128, 2048], P('rhs', 'leaf'), may hold values from -0.75 to 0.75
- obs_data: float32 [320, 2048], P('rhs', 'leaf'), may hold values from -6 to 6
- obs_target: int32 [2048], P('leaf'), may hold values from 0 to 31, as said below
- leaf_map: int32 [32], replicated, may hold values from 0 to 31, as said below
- leaf_parent: int32 [32], replicated, may hold values from 0 to 7
- leaf_inv: float32 [32, 128, 128], P('leaf'), may hold values from -0.5 to 1.5
- leaf_off: float32 [32, 128, 128], P('leaf'), may hold values from -0.25 to 0.25
- top_inv: float32 [8, 128, 128], replicated, may hold values from -0.5 to 1.5
- top_rhs: float32 [8, 320, 128], P(None, 'rhs'), may hold values from -6 to 6
Outputs:
- leaf_solution: float32 [32, 320, 128], P('leaf', 'rhs')
- top_solution: float32 [8, 320, 128], P(None, 'rhs')
Inputs may be any that keep to these rules, and one draw needn't show every extreme that they name: A permutation: supernode i is stored at position leaf_map[i], which lies on index leaf_map[i] // 4 of leaf. `obs_target`: the rows held by one index of leaf name supernodes stored on any one index of leaf at most 64 times; in every draw one index of leaf is named exactly 64 times by the rows of every index.
All inputs are finite; a program needn't handle non-finite values.
Results may differ from a plain program's by a relative error of at most 0.0003.
Values sent between devices are 32-bit elements; how exact they have to be, the bound alone decides.
A program may use at most 64 MiB of HBM per device.

v0:
```python
import jax
import jax.numpy as jnp
from jax import lax
from jax.sharding import PartitionSpec as P


def body(
    obs_coef, obs_data, obs_target, leaf_map, leaf_parent, leaf_inv, leaf_off, top_inv, top_rhs
):
    highest = lax.Precision.HIGHEST
    groups = lax.axis_size("leaf")
    device_index = lax.axis_index("leaf")
    local_count = leaf_inv.shape[0]
    block_width = leaf_inv.shape[1]
    top_count = top_inv.shape[0]
    date_cols = obs_data.shape[0]
    rows_here = obs_target.shape[0]
    leaf_total = leaf_map.shape[0]
    capacity = max(2, 2 * rows_here // groups)
    slots_total = groups * capacity
    all_ids = jnp.arange(leaf_total, dtype=jnp.int32)
    id_match = obs_target[:, None] == all_ids[None, :]
    position = jnp.sum(jnp.where(id_match, leaf_map[None, :], 0), axis=1)
    owner_dev = position // local_count
    member = position % local_count
    row_ids = jnp.arange(rows_here, dtype=jnp.int32)
    earlier = (owner_dev[:, None] == owner_dev[None, :]) & (row_ids[:, None] > row_ids[None, :])
    queue_rank = jnp.sum(earlier.astype(jnp.int32), axis=1)
    target_slot = owner_dev * capacity + queue_rank
    slot_mark = (member + 1).astype(jnp.float32)[None, :]

    def place_rows(values):
        return jnp.zeros((values.shape[0], slots_total), jnp.float32).at[:, target_slot].set(values)

    part_coef, recv_data, recv_mark = (
        lax.all_to_all(place_rows(obs_coef), "leaf", split_axis=1, concat_axis=1, tiled=True),
        lax.all_to_all(place_rows(obs_data), "leaf", split_axis=1, concat_axis=1, tiled=True),
        lax.all_to_all(place_rows(slot_mark), "leaf", split_axis=1, concat_axis=1, tiled=True),
    )
    recv_coef = lax.all_gather(part_coef, "rhs", axis=0, tiled=True)
    slot_values = (jnp.arange(local_count, dtype=jnp.int32) + 1).astype(jnp.float32)
    chosen = (recv_mark[0][None, :] == slot_values[:, None]).astype(jnp.float32)
    spread = (recv_data[None, :, :] * chosen[:, None, :]).reshape(
        local_count * date_cols, slots_total
    )
    leaf_rhs = lax.dot_general(
        spread, recv_coef, (((1,), (1,)), ((), ())), precision=highest
    ).reshape(local_count, date_cols, block_width)
    solved = jnp.einsum("ltc,ldc->ltd", leaf_rhs, leaf_inv, precision=highest)
    update = jnp.einsum("ltd,lcd->ltc", solved, leaf_off, precision=highest)
    positions_here = device_index * local_count + jnp.arange(local_count, dtype=jnp.int32)
    holder_match = leaf_map[None, :] == positions_here[:, None]
    parent_here = jnp.sum(jnp.where(holder_match, leaf_parent[None, :], 0), axis=1)
    to_top = (parent_here[:, None] == jnp.arange(top_count, dtype=jnp.int32)[None, :]).astype(
        jnp.float32
    )
    contrib = jnp.einsum("lp,ltc->ptc", to_top, update, precision=highest)
    flat_terms = contrib.reshape(top_count * date_cols, block_width)
    top_total = lax.psum(flat_terms, "leaf").reshape(top_count, date_cols, block_width)
    residue = top_rhs - top_total
    top_solved = jnp.einsum("ptc,pdc->ptd", residue, top_inv, precision=highest)
    top_solution = jnp.einsum("ptd,pdc->ptc", top_solved, top_inv, precision=highest)
    from_top = jnp.einsum("lp,ptc->ltc", to_top, top_solution, precision=highest)
    lifted = jnp.einsum("ltc,lcd->ltd", from_top, leaf_off, precision=highest)
    leaf_solution = jnp.einsum("ltc,lcd->ltd", solved - lifted, leaf_inv, precision=highest)
    return (leaf_solution, top_solution)


def solution(mesh):
    return jax.shard_map(
        body,
        mesh=mesh,
        in_specs=(
            P("rhs", "leaf"),
            P("rhs", "leaf"),
            P("leaf"),
            P(),
            P(),
            P("leaf", None, None),
            P("leaf", None, None),
            P(),
            P(None, "rhs", None),
        ),
        out_specs=(P("leaf", "rhs", None), P(None, "rhs", None)),
        check_vma=False,
    )
```

profile of v0, /device:TPU:0, one launch (start us, length us, event | category | flops | bytes accessed | tf_op | source)
XLA Modules:
  0.0 132.9 jit_solution(14275067791742011380)
XLA Ops:
  7.2 0.8 select_reduce_fusion
  8.3 1.4 %scatter_custom_fusion.1 = f32[512]{0:T(512)S(1)} fusion(s32[256]{0:T(256)S(1)} %bitcast.42, f32[256]{0:T(256)S(1)} %bitcast.45, f32[]{:T(128)} %constant.35.clone.1), kind=kCustom, calls=%fused_computation.45 | custom fusion | bytes 2052 | tf_op jit(solution)/shard_map/scatter | solution.py:33
  9.7 0.7 all_to_all.22
  10.3 7.3 %all-to-all-start.1 = ((f32[1,8,64]{2,0,1:T(1,128)}), f32[1,8,64]{2,0,1:T(1,128)S(1)}, u32[]{:S(2)}, u32[]{:S(2)}) async-start(f32[1,8,64]{2,0,1:T(1,128)} %all_to_all.22), calls=%async_computation.1 | async-start | bytes 8192 | tf_op jit(solution)/shard_map/all_to_all | solution.py:38
  17.7 1.2 scatter_custom_fusion.2
  19.1 0.8 reshape.240
  19.9 4.2 %all-to-all-done.1 = f32[1,8,64]{2,0,1:T(1,128)S(1)} async-done(((f32[1,8,64]{2,0,1:T(1,128)}), f32[1,8,64]{2,0,1:T(1,128)S(1)}, u32[]{:S(2)}, u32[]{:S(2)}) %all-to-all-start.1) | async-done | bytes 2080 | tf_op jit(solution)/shard_map/all_to_all | solution.py:38
  24.0 3.4 %all-to-all-start.2 = ((f32[8,1,2048]{2,1,0:T(1,128)}), f32[8,1,2048]{2,1,0:T(1,128)S(1)}, u32[]{:S(2)}, u32[]{:S(2)}) async-start(f32[8,1,2048]{2,1,0:T(1,128)} %reshape.240), calls=%async_computation.2 | async-start | bytes 131072 | tf_op jit(solution)/shard_map/all_to_all | solution.py:36
  27.5 1.8 %scatter_custom_fusion = f32[80,512]{0,1:T(8,128)} fusion(s32[256]{0:T(256)S(1)} %bitcast.44, f32[256,80]{1,0:T(8,128)S(1)} %copy.36, f32[]{:T(128)} %constant.35.clone.1), kind=kCustom, calls=%fused_computation.22 | custom fusion | bytes 163844 | tf_op jit(solution)/shard_map/scatter | solution.py:33
  30.1 0.7 reduce.3
  30.9 3.3 %all-to-all-done.2 = f32[8,1,2048]{2,1,0:T(1,128)S(1)} async-done(((f32[8,1,2048]{2,1,0:T(1,128)}), f32[8,1,2048]{2,1,0:T(1,128)S(1)}, u32[]{:S(2)}, u32[]{:S(2)}) %all-to-all-start.2) | async-done | bytes 65568 | tf_op jit(solution)/shard_map/all_to_all | solution.py:36
  34.2 3.4 %all-to-all-start = ((f32[80,8,64]{0,2,1:T(8,128)}), f32[80,8,64]{0,2,1:T(8,128)S(1)}, u32[]{:S(2)}, u32[]{:S(2)}) async-start(f32[80,8,64]{0,2,1:T(8,128)} %bitcast.4), calls=%async_computation | async-start | bytes 524288 | tf_op jit(solution)/shard_map/all_to_all | solution.py:37
  38.3 0.8 reduce.4
  39.3 5.8 %all_gather.3 = f32[128,512]{1,0:T(8,128)S(1)} all-gather(f32[32,512]{1,0:T(8,128)S(1)} %all_to_all.26), channel_id=1, replica_groups=mesh['leaf'=8,'rhs'=4] {'rhs'}, dimensions={0}, use_global_device_ids=true | all-gather | bytes 327680 | tf_op jit(solution)/shard_map/all_gather | solution.py:40
  45.1 0.7 all-to-all-done
  45.9 0.7 fusion
  46.9 0.6 fusion.27
  47.8 0.6 fusion.28
  48.5 1.1 fusion.11
  49.6 71.8 %all-reduce.2.cloned.1.call-done = f32[8,80,128]{2,0,1:T(8,128)} async-done(((f32[8,80,128]{2,0,1:T(8,128)}), f32[8,80,128]{2,0,1:T(8,128)}) %all-reduce.2.cloned.1.call-update) | async-done | bytes 327696 | tf_op jit(solution)/shard_map/psum | solution.py:59
  121.4 1.1 copy_subtract_fusion
  122.5 1.1 fusion.4
  123.7 0.6 fusion.29
  125.1 1.0 fusion.30
  (40 shorter events, 3.8 us)
Async XLA Ops:
  7.2 115.3 %copy-start = (f32[8,128,128]{2,1,0:T(8,128)S(1)}, f32[8,128,128]{2,1,0:T(8,128)}, u32[]{:S(2)}) copy-start(f32[8,128,128]{2,1,0:T(8,128)} %param.16) | copy-start | bytes 1572868
  7.2 10.5 %copy-start.6 = (f32[32,256]{1,0:T(8,128)S(1)}, f32[32,256]{1,0:T(8,128)}, u32[]{:S(2)}) copy-start(f32[32,256]{1,0:T(8,128)} %param.9) | copy-start | bytes 98308
  10.3 13.7 %all-to-all-start.1 = ((f32[1,8,64]{2,0,1:T(1,128)}), f32[1,8,64]{2,0,1:T(1,128)S(1)}, u32[]{:S(2)}, u32[]{:S(2)}) async-start(f32[1,8,64]{2,0,1:T(1,128)} %all_to_all.22), calls=%async_computation.1 | async-start | bytes 8192 | tf_op jit(solution)/shard_map/all_to_all | solution.py:38
  19.9 7.5 %copy-start.5 = (f32[80,256]{1,0:T(8,128)S(1)}, f32[80,256]{1,0:T(8,128)}, u32[]{:S(2)}) copy-start(f32[80,256]{1,0:T(8,128)} %param.10) | copy-start | bytes 245764
  24.0 10.2 %all-to-all-start.2 = ((f32[8,1,2048]{2,1,0:T(1,128)}), f32[8,1,2048]{2,1,0:T(1,128)S(1)}, u32[]{:S(2)}, u32[]{:S(2)}) async-start(f32[8,1,2048]{2,1,0:T(1,128)} %reshape.240), calls=%async_computation.2 | async-start | bytes 131072 | tf_op jit(solution)/shard_map/all_to_all | solution.py:36
  27.5 1.8 %copy-start.7 = (s32[32]{0:T(128)S(1)}, s32[32]{0:T(128)}, u32[]{:S(2)}) copy-start(s32[32]{0:T(128)} %param.12) | copy-start | bytes 388
  27.5 1.8 %copy-start.8 = (s32[32]{0:T(128)S(1)}, s32[32]{0:T(128)}, u32[]{:S(2)}) copy-start(s32[32]{0:T(128)} %param.13) | copy-start | bytes 388
  34.2 11.6 %all-to-all-start = ((f32[80,8,64]{0,2,1:T(8,128)}), f32[80,8,64]{0,2,1:T(8,128)S(1)}, u32[]{:S(2)}, u32[]{:S(2)}) async-start(f32[80,8,64]{0,2,1:T(8,128)} %bitcast.4), calls=%async_computation | async-start | bytes 524288 | tf_op jit(solution)/shard_map/all_to_all | solution.py:37
  37.6 83.8 %all-reduce.2.cloned.1.call-start = ((), (), s32[]{:S(2)}) async-start(), calls=%async_computation.3 | async-start | bytes 655360 | tf_op jit(solution)/shard_map/psum | solution.py:59
  45.9 1.0 copy-start.3
  46.9 0.9 copy-start.2
  48.4 73.0 %copy-start.4 = (f32[8,80,128]{2,1,0:T(8,128)S(1)}, f32[8,80,128]{2,1,0:T(8,128)}, u32[]{:S(2)}) copy-start(f32[8,80,128]{2,1,0:T(8,128)} %param.17) | copy-start | bytes 983044
  124.3 0.8 copy-start.1
Sparse Core Ops, SparseCore 0:
  49.7 71.6 all-reduce.1
where the time goes:
time: 133 us
  waiting for transfers between devices  80 us (60%)
  between operations  14.3 us (11%)
  starting transfers between devices  14.1 us (11%)
  local copies, waits for them, and re-layouts  8.35 us (6%)
  matrix products  6.57 us (5%)
  blocking collectives  5.79 us (4%)
  other arithmetic  3.91 us (3%)
    psum x1, waiting for transfers between devices, body(): lax.psum(flat_terms, 'leaf').reshape(top_count, date_cols, block_width)  71.8 us
    all_to_all x1, starting transfers between devices, body(): lax.all_to_all(place_rows(slot_mark), 'leaf', split_axis=1, concat_axis=1...  7.28 us
    all_gather x1, blocking collectives, body(): recv_coef = lax.all_gather(part_coef, 'rhs', axis=0, tiled=True)  5.79 us
    scatter x3, local copies, waits for them, and re-layouts, place_rows(): jnp.zeros((values.shape[0], slots_total), jnp.float32).at[:, target_slot]  4.43 us
    all_to_all x1, waiting for transfers between devices, body(): lax.all_to_all(place_rows(slot_mark), 'leaf', split_axis=1, concat_axis=1...  4.16 us
    all_to_all x1, starting transfers between devices, body(): lax.all_to_all(place_rows(obs_data), 'leaf', split_axis=1, concat_axis=1,...  3.41 us
    all_to_all x1, starting transfers between devices, body(): lax.all_to_all(place_rows(obs_coef), 'leaf', split_axis=1, concat_axis=1,...  3.35 us
    all_to_all x1, waiting for transfers between devices, body(): lax.all_to_all(place_rows(obs_coef), 'leaf', split_axis=1, concat_axis=1,...  3.31 us
  transfers between devices with their start and end apart: 4, of which 4 were waited for; matrix products, arithmetic and copies ran while one was open for 5% of the time, Pallas kernels for 0%

commit v1 on v0

--- a/solution.py
+++ b/solution.py
@@ -1,10 +1,280 @@
+import functools
+
 import jax
 import jax.numpy as jnp
 from jax import lax
+from jax.experimental import pallas as pl
+from jax.experimental.pallas import tpu as pltpu
 from jax.sharding import PartitionSpec as P
 
-
-def body(
+F32, BF16 = jnp.float32, jnp.bfloat16
+MESH = pl.DeviceIdType.MESH
+LANES = 128
+
+
+def split(x):
+    high = x.astype(BF16)
+    return high, (x - high.astype(F32)).astype(BF16)
+
+
+def contract(a, b, ca, cb):
+    return lax.dot_general(a, b, (((ca,), (cb,)), ((), ())), preferred_element_type=F32)
+
+
+def dot3(a, b, ca, cb):
+    (ah, al), (bh, bl) = a, b
+    return contract(ah, bh, ca, cb) + (contract(ah, bl, ca, cb) + contract(al, bh, ca, cb))
+
+
+def kernel(
+    groups, shards, capacity,
+    tgt, coef, data, lmap, lpar, inv, off, tinv, trhs,
+    leaf_out, top_out,
+    send, recv, packed, wide, base, parts, arrived, tinv_v, trhs_v,
+    d_send, d_recv, f_send, f_recv, r_send, r_recv, g_send, g_recv, l_sem,
+):
+    me = lax.axis_index("leaf")
+    shard = lax.axis_index("rhs")
+    local, width = inv.shape[0], inv.shape[1]
+    coef_rows, rows = coef.shape
+    dates = data.shape[0]
+    top_each = tinv_v.shape[0]
+    total = lmap.shape[0]
+    fold = LANES // coef_rows
+    piece = capacity // fold
+    pair = f_send.shape[1]
+    per = groups // pair
+    leaf_peers = [lax.rem(me + o, groups) for o in range(groups)]
+    rhs_peers = [lax.rem(shard + o, shards) for o in range(shards)]
+
+    barrier = pltpu.get_barrier_semaphore()
+    for o in range(1, groups):
+        pl.semaphore_signal(barrier, inc=1, device_id=(leaf_peers[o], shard), device_id_type=MESH)
+    for o in range(1, shards):
+        pl.semaphore_signal(barrier, inc=1, device_id=(me, rhs_peers[o]), device_id_type=MESH)
+    tops = pl.ds(me * top_each, top_each)
+    load_inv = pltpu.make_async_copy(tinv.at[tops], tinv_v, l_sem.at[0])
+    load_rhs = pltpu.make_async_copy(trhs.at[tops], trhs_v, l_sem.at[1])
+    load_inv.start()
+    load_rhs.start()
+
+    target = tgt[...]
+    position = jnp.zeros_like(target)
+    for i in range(total):
+        position = jnp.where(target == i, lmap[i], position)
+    first = lax.broadcasted_iota(jnp.int32, (groups, rows), 0) * local
+    member = jnp.broadcast_to(position, (groups, rows)) - first
+    owned = (member >= 0) & (member < local)
+    hot = jnp.where(owned, 1.0, 0.0)
+    before = (
+        lax.broadcasted_iota(jnp.int32, (rows, rows), 0)
+        < lax.broadcasted_iota(jnp.int32, (rows, rows), 1)
+    )
+    rank = contract(hot.astype(BF16), jnp.where(before, 1.0, 0.0).astype(BF16), 1, 0)
+    slot = jnp.where(owned, rank.astype(jnp.int32), -1)
+    mark = jnp.sum(hot * (member + 1).astype(F32), axis=0, keepdims=True)
+    slot_ids = lax.broadcasted_iota(jnp.int32, (capacity, rows), 0)
+    chosen = jnp.concatenate(
+        [jnp.where(slot_ids == slot[d : d + 1, :], 1.0, 0.0) for d in range(groups)], axis=0
+    ).astype(BF16)
+    fields = jnp.concatenate(
+        [
+            coef[...],
+            data[...],
+            jnp.broadcast_to(mark, (LANES - coef_rows - dates, rows)),
+        ],
+        axis=0,
+    )
+    high, low = split(fields)
+    payload = contract(chosen, high, 1, 1) + contract(chosen, low, 1, 1)
+    send[...] = payload.reshape(groups, capacity, LANES)
+
+    pl.semaphore_wait(barrier, groups - 1 + shards - 1)
+    row_copies = []
+    for o in range(1, groups):
+        copy = pltpu.make_async_remote_copy(
+            src_ref=send.at[leaf_peers[o]],
+            dst_ref=recv.at[o],
+            send_sem=d_send.at[o],
+            recv_sem=d_recv.at[o],
+            device_id=(leaf_peers[o], shard),
+            device_id_type=MESH,
+        )
+        copy.start()
+        row_copies.append(copy)
+    recv[0] = send[me]
+
+    for l in range(local):
+        high, low = split(dot3(split(off[l]), split(inv[l]), 1, 0))
+        wide[0, l] = high
+        wide[1, l] = low
+    load_inv.wait()
+    load_rhs.wait()
+    gram = []
+    for i in range(top_each):
+        block = split(tinv_v[i])
+        gram.append(split(dot3(block, block, 0, 0)))
+    up = []
+    for l in range(local):
+        found = jnp.int32(0)
+        for i in range(total):
+            found = jnp.where(lmap[i] == me * local + l, lpar[i], found)
+        up.append(found)
+
+    lane_group = lax.broadcasted_iota(jnp.int32, (piece, LANES), 1) // coef_rows
+    forwards = []
+    for g in range(pair):
+        for o in range(g * per, (g + 1) * per):
+            if o > 0:
+                row_copies[o - 1].wait_recv()
+            block = recv[o]
+            out = block[:piece]
+            for q in range(1, fold):
+                moved = pltpu.roll(block[q * piece : (q + 1) * piece], q * coef_rows, 1)
+                out = jnp.where(lane_group == q, moved, out)
+            packed[shard, o] = out
+        span = pl.ds(g * per, per)
+        for o in range(1, shards):
+            copy = pltpu.make_async_remote_copy(
+                src_ref=packed.at[shard, span],
+                dst_ref=packed.at[shard, span],
+                send_sem=f_send.at[o, g],
+                recv_sem=f_recv.at[o, g],
+                device_id=(me, rhs_peers[o]),
+                device_id_type=MESH,
+            )
+            copy.start()
+            forwards.append(copy)
+    slots = groups * capacity
+    rows_in = recv[...].reshape(slots, LANES)
+    turned = split(rows_in.T)
+    marks = rows_in[:, coef_rows + dates : coef_rows + dates + 1]
+    for copy in forwards:
+        copy.wait_recv()
+
+    packs = [packed[s].reshape(groups * piece, LANES) for s in range(shards)]
+    big_group = lax.broadcasted_iota(jnp.int32, (groups * piece, LANES), 1) // coef_rows
+    pieces = []
+    for q in range(fold):
+        out = None
+        for s in range(shards):
+            shift = ((s - q) * coef_rows) % LANES
+            moved = pltpu.roll(packs[s], shift, 1) if shift else packs[s]
+            out = moved if out is None else jnp.where(big_group == s, moved, out)
+        pieces.append(out.reshape(groups, 1, piece, LANES))
+    coefs = jnp.concatenate(pieces, axis=1).reshape(slots, LANES)
+    spread = jnp.concatenate(
+        [jnp.where(marks == float(l + 1), coefs, 0.0) for l in range(local)], axis=1
+    )
+    rhs_all = dot3(turned, split(spread), 1, 0)[coef_rows : coef_rows + dates]
+    rhs = [split(rhs_all[:, l * width : (l + 1) * width]) for l in range(local)]
+    updates = [dot3(rhs[l], (wide[0, l], wide[1, l]), 1, 1) for l in range(local)]
+    tops_all = top_out.shape[0]
+    for p in range(tops_all):
+        acc = None
+        for l in range(local):
+            term = jnp.where(up[l] == p, 1.0, 0.0) * updates[l]
+            acc = term if acc is None else acc + term
+        parts[p] = acc
+    sums = []
+    for o in range(1, groups):
+        copy = pltpu.make_async_remote_copy(
+            src_ref=parts.at[pl.ds(leaf_peers[o] * top_each, top_each)],
+            dst_ref=arrived.at[o],
+            send_sem=r_send.at[o],
+            recv_sem=r_recv.at[o],
+            device_id=(leaf_peers[o], shard),
+            device_id_type=MESH,
+        )
+        copy.start()
+        sums.append(copy)
+    for l in range(local):
+        factor = split(inv[l])
+        solved = split(dot3(rhs[l], factor, 1, 1))
+        base[l] = dot3(solved, factor, 1, 0)
+    residue = [trhs_v[i] - parts[me * top_each + i] for i in range(top_each)]
+    for o in range(1, groups):
+        sums[o - 1].wait_recv()
+        residue = [residue[i] - arrived[o, i] for i in range(top_each)]
+    for i in range(top_each):
+        top_out[me * top_each + i] = dot3(split(residue[i]), gram[i], 1, 0)
+    solutions = []
+    for o in range(1, groups):
+        copy = pltpu.make_async_remote_copy(
+            src_ref=top_out.at[tops],
+            dst_ref=top_out.at[tops],
+            send_sem=g_send.at[o],
+            recv_sem=g_recv.at[o],
+            device_id=(leaf_peers[o], shard),
+            device_id_type=MESH,
+        )
+        copy.start()
+        solutions.append(copy)
+    for copy in row_copies + forwards + sums:
+        copy.wait_send()
+    for copy in solutions:
+        copy.wait_recv()
+    for l in range(local):
+        lifted = dot3(split(top_out[up[l]]), (wide[0, l], wide[1, l]), 1, 0)
+        leaf_out[l] = base[l] - lifted
+    for copy in solutions:
+        copy.wait_send()
+
+
+def fused(
+    obs_coef, obs_data, obs_target, leaf_map, leaf_parent, leaf_inv, leaf_off, top_inv, top_rhs
+):
+    groups, shards = lax.axis_size("leaf"), lax.axis_size("rhs")
+    rows = obs_target.shape[0]
+    capacity = 2 * rows // groups
+    local, width = leaf_inv.shape[0], leaf_inv.shape[1]
+    top_count, dates = top_inv.shape[0], obs_data.shape[0]
+    top_each = top_count // groups
+    coef_rows = obs_coef.shape[0]
+    piece = capacity * coef_rows // LANES
+    pair = groups // 2 if groups % 2 == 0 else groups
+    dma = pltpu.SemaphoreType.DMA
+    vmem = pl.BlockSpec(memory_space=pltpu.VMEM)
+    smem = pl.BlockSpec(memory_space=pltpu.SMEM)
+    hbm = pl.BlockSpec(memory_space=pl.ANY)
+    return pl.pallas_call(
+        functools.partial(kernel, groups, shards, capacity),
+        out_shape=(
+            jax.ShapeDtypeStruct((local, dates, width), F32),
+            jax.ShapeDtypeStruct((top_count, dates, width), F32),
+        ),
+        in_specs=[vmem, vmem, vmem, smem, smem, vmem, vmem, hbm, hbm],
+        out_specs=(vmem, vmem),
+        scratch_shapes=[
+            pltpu.VMEM((groups, capacity, LANES), F32),
+            pltpu.VMEM((groups, capacity, LANES), F32),
+            pltpu.VMEM((shards, groups, piece, LANES), F32),
+            pltpu.VMEM((2, local, width, width), BF16),
+            pltpu.VMEM((local, dates, width), F32),
+            pltpu.VMEM((top_count, dates, width), F32),
+            pltpu.VMEM((groups, top_each, dates, width), F32),
+            pltpu.VMEM((top_each, width, width), F32),
+            pltpu.VMEM((top_each, dates, width), F32),
+            dma((groups,)),
+            dma((groups,)),
+            dma((shards, pair)),
+            dma((shards, pair)),
+            dma((groups,)),
+            dma((groups,)),
+            dma((groups,)),
+            dma((groups,)),
+            dma((2,)),
+        ],
+        compiler_params=pltpu.CompilerParams(
+            collective_id=0, has_side_effects=True, vmem_limit_bytes=24 * 2**20
+        ),
+    )(
+        obs_target.reshape(1, rows), obs_coef, obs_data, leaf_map, leaf_parent,
+        leaf_inv, leaf_off, top_inv, top_rhs,
+    )
+
+
+def plain(
     obs_coef, obs_data, obs_target, leaf_map, leaf_parent, leaf_inv, leaf_off, top_inv, top_rhs
 ):
     highest = lax.Precision.HIGHEST
@@ -28,15 +298,12 @@
     queue_rank = jnp.sum(earlier.astype(jnp.int32), axis=1)
     target_slot = owner_dev * capacity + queue_rank
     slot_mark = (member + 1).astype(jnp.float32)[None, :]
-
-    def place_rows(values):
-        return jnp.zeros((values.shape[0], slots_total), jnp.float32).at[:, target_slot].set(values)
-
-    part_coef, recv_data, recv_mark = (
-        lax.all_to_all(place_rows(obs_coef), "leaf", split_axis=1, concat_axis=1, tiled=True),
-        lax.all_to_all(place_rows(obs_data), "leaf", split_axis=1, concat_axis=1, tiled=True),
-        lax.all_to_all(place_rows(slot_mark), "leaf", split_axis=1, concat_axis=1, tiled=True),
-    )
+    fields = jnp.concatenate([obs_coef, obs_data, slot_mark], axis=0)
+    placed = jnp.zeros((fields.shape[0], slots_total), F32).at[:, target_slot].set(fields)
+    received = lax.all_to_all(placed, "leaf", split_axis=1, concat_axis=1, tiled=True)
+    part_coef = received[: obs_coef.shape[0]]
+    recv_data = received[obs_coef.shape[0] : -1]
+    recv_mark = received[-1:]
     recv_coef = lax.all_gather(part_coef, "rhs", axis=0, tiled=True)
     slot_values = (jnp.arange(local_count, dtype=jnp.int32) + 1).astype(jnp.float32)
     chosen = (recv_mark[0][None, :] == slot_values[:, None]).astype(jnp.float32)
@@ -64,6 +331,25 @@
     lifted = jnp.einsum("ltc,lcd->ltd", from_top, leaf_off, precision=highest)
     leaf_solution = jnp.einsum("ltc,lcd->ltd", solved - lifted, leaf_inv, precision=highest)
     return (leaf_solution, top_solution)
+
+
+def body(*args):
+    obs_coef, obs_data, obs_target = args[:3]
+    groups = lax.axis_size("leaf")
+    coef_rows, rows = obs_coef.shape
+    dates = obs_data.shape[0]
+    fits = (
+        args[7].shape[0] % groups == 0
+        and rows % LANES == 0
+        and (2 * rows) % groups == 0
+        and LANES % coef_rows == 0
+        and (2 * rows // groups) % (8 * (LANES // coef_rows)) == 0
+        and coef_rows % 8 == 0
+        and dates % 8 == 0
+        and coef_rows + dates < LANES
+        and args[5].shape[1] == LANES
+    )
+    return fused(*args) if fits else plain(*args)
 
 
 def solution(mesh):

time: 133 us -> 43.6 us (0.33)
  waiting for transfers between devices: 80 us -> 0 us
  Pallas kernels: 0 us -> 34.2 us
  starting transfers between devices: 14.1 us -> 0 us
  between operations: 14.3 us -> 0.67 us
  matrix products: 6.57 us -> 0 us
  blocking collectives: 5.79 us -> 0 us
  other arithmetic: 3.91 us -> 0 us
    psum x1 -> x0, waiting for transfers between devices: 71.8 us -> none  [body(): lax.psum(flat_terms, 'leaf').reshape(top_count, date_cols, block_width)]
    pallas_call x0 -> x1, Pallas kernels: none -> 34.2 us  [fused(): pl.pallas_call(functools.partial(kernel, groups, shards, capacity), out_s...]
    all_to_all x3 -> x0, starting transfers between devices: 14 us -> none  [the longest x1 7.28 us: body(): lax.all_to_all(place_rows(slot_mark), 'leaf', split_axis=1, concat_axis=1...]
    all_to_all x3 -> x0, waiting for transfers between devices: 8.14 us -> none  [the longest x1 4.16 us: body(): lax.all_to_all(place_rows(slot_mark), 'leaf', split_axis=1, concat_axis=1...]
    unnamed x22 -> x20, local copies, waits for them, and re-layouts: 1.66 us -> 8.28 us
    dot_general x9 -> x0, matrix products: 6.57 us -> none  [the longest x1 1.13 us: body(): top_solved = jnp.einsum('ptc,pdc->ptd', residue, top_inv, precision=highest)]
    all_gather x1 -> x0, blocking collectives: 5.79 us -> none  [body(): recv_coef = lax.all_gather(part_coef, 'rhs', axis=0, tiled=True)]
    scatter x3 -> x0, local copies, waits for them, and re-layouts: 4.43 us -> none  [place_rows(): jnp.zeros((values.shape[0], slots_total), jnp.float32).at[:, target_slot]]
  transfers between devices with their start and end apart: 4 -> 0, of which waited for: 4 -> 0; matrix products, arithmetic and copies ran while one was open for 5% -> 0% of each run, Pallas kernels for 0% -> 0%
where the time goes in v1:
time: 43.6 us; the launch traced here: 43.2 us
  Pallas kernels  34.2 us (78%)
  local copies, waits for them, and re-layouts  8.28 us (19%)
  between operations  0.67 us (2%)
    pallas_call x1, Pallas kernels, fused(): pl.pallas_call(functools.partial(kernel, groups, shards, capacity), out_s...  34.2 us
    unnamed x20, local copies, waits for them, and re-layouts  8.28 us

profile of v1, /device:TPU:0, one launch (start us, length us, event | category | flops | bytes accessed | tf_op | source)
XLA Modules:
  0.0 43.2 jit_solution(7286549091049254954)
XLA Ops:
  0.6 0.0 copy-start.7
  0.6 0.0 copy-start.6
  0.7 0.6 %copy-done.7 = s32[32]{0:T(128)S(1)} copy-done((s32[32]{0:T(128)S(1)}, s32[32]{0:T(128)}, u32[]{:S(2)}) %copy-start.7) | copy-done | bytes 152
  1.3 0.0 copy-done.6
  1.3 0.0 copy-start
  1.3 1.0 %copy-done = f32[8,128,128]{2,1,0:T(8,128)S(1)} copy-done((f32[8,128,128]{2,1,0:T(8,128)S(1)}, f32[8,128,128]{2,1,0:T(8,128)}, u32[]{:S(2)}) %copy-start) | copy-done | bytes 524312
  2.4 0.0 copy-start.1
  2.4 1.0 %copy-done.1 = f32[8,80,128]{2,1,0:T(8,128)S(1)} copy-done((f32[8,80,128]{2,1,0:T(8,128)S(1)}, f32[8,80,128]{2,1,0:T(8,128)}, u32[]{:S(2)}) %copy-start.1) | copy-done | bytes 327704
  3.3 0.0 copy-start.2
  3.3 0.9 %copy-done.2 = f32[4,128,128]{2,1,0:T(8,128)S(1)} copy-done((f32[4,128,128]{2,1,0:T(8,128)S(1)}, f32[4,128,128]{2,1,0:T(8,128)}, u32[]{:S(2)}) %copy-start.2) | copy-done | bytes 262168
  4.3 0.0 copy-start.3
  4.3 0.9 %copy-done.3 = f32[4,128,128]{2,1,0:T(8,128)S(1)} copy-done((f32[4,128,128]{2,1,0:T(8,128)S(1)}, f32[4,128,128]{2,1,0:T(8,128)}, u32[]{:S(2)}) %copy-start.3) | copy-done | bytes 262168
  5.2 0.0 copy-start.4
  5.2 0.9 %copy-done.4 = f32[80,256]{1,0:T(8,128)S(1)} copy-done((f32[80,256]{1,0:T(8,128)S(1)}, f32[80,256]{1,0:T(8,128)}, u32[]{:S(2)}) %copy-start.4) | copy-done | bytes 81944
  6.1 0.0 copy-start.5
  6.1 0.8 %copy-done.5 = f32[32,256]{1,0:T(8,128)S(1)} copy-done((f32[32,256]{1,0:T(8,128)S(1)}, f32[32,256]{1,0:T(8,128)}, u32[]{:S(2)}) %copy-start.5) | copy-done | bytes 32792
  6.9 0.0 copy-start.8
  6.9 0.7 %copy-done.8 = s32[32]{0:T(128)S(1)} copy-done((s32[32]{0:T(128)S(1)}, s32[32]{0:T(128)}, u32[]{:S(2)}) %copy-start.8) | copy-done | bytes 152
  7.5 34.2 %shard_map.104 = (f32[4,80,128]{2,1,0:T(8,128)S(1)}, f32[8,80,128]{2,1,0:T(8,128)S(1)}) custom-call(s32[1,256]{1,0:T(1,128)S(1)} %bitcast.1, f32[32,256]{1,0:T(8,128)S(1)} %copy-done.5, f32[80,256]{1,0:T(8,128)S(1)} %copy-done.4, s32[32]{0:T(128)S(1)} %copy-done.7, s32[32]{0:T(128)S(1)} %copy-done.8, f32[4,128,128]{2,1,0:T(8,128)S(1)} %copy-done.2, ...), custom_call_target="tpu_custom_call" | custom-call | tf_op jit(solution)/shard_map/pallas_call | solution.py:240
  41.8 0.7 %copy.13 = f32[4,80,128]{2,1,0:T(8,128)} copy(f32[4,80,128]{2,1,0:T(8,128)S(1)} %get-tuple-element.4) | data formatting | bytes 327680
  42.5 0.7 %copy.14 = f32[8,80,128]{2,1,0:T(8,128)} copy(f32[8,80,128]{2,1,0:T(8,128)S(1)} %get-tuple-element.5) | data formatting | bytes 655360
Async XLA Ops:
  0.6 0.7 %copy-start.7 = (s32[32]{0:T(128)S(1)}, s32[32]{0:T(128)}, u32[]{:S(2)}) copy-start(s32[32]{0:T(128)} %lmap.1) | copy-start | bytes 388
  0.6 0.7 %copy-start.6 = (s32[256]{0:T(256)S(1)}, s32[256]{0:T(256)}, u32[]{:S(2)}) copy-start(s32[256]{0:T(256)} %param.11) | copy-start | bytes 3076
  1.3 1.0 %copy-start = (f32[8,128,128]{2,1,0:T(8,128)S(1)}, f32[8,128,128]{2,1,0:T(8,128)}, u32[]{:S(2)}) copy-start(f32[8,128,128]{2,1,0:T(8,128)} %tinv.1) | copy-start | bytes 1572868
  2.4 1.0 %copy-start.1 = (f32[8,80,128]{2,1,0:T(8,128)S(1)}, f32[8,80,128]{2,1,0:T(8,128)}, u32[]{:S(2)}) copy-start(f32[8,80,128]{2,1,0:T(8,128)} %trhs.1) | copy-start | bytes 983044
  3.3 0.9 %copy-start.2 = (f32[4,128,128]{2,1,0:T(8,128)S(1)}, f32[4,128,128]{2,1,0:T(8,128)}, u32[]{:S(2)}) copy-start(f32[4,128,128]{2,1,0:T(8,128)} %inv.1) | copy-start | bytes 786436
  4.3 0.9 %copy-start.3 = (f32[4,128,128]{2,1,0:T(8,128)S(1)}, f32[4,128,128]{2,1,0:T(8,128)}, u32[]{:S(2)}) copy-start(f32[4,128,128]{2,1,0:T(8,128)} %off.1) | copy-start | bytes 786436
  5.2 0.9 %copy-start.4 = (f32[80,256]{1,0:T(8,128)S(1)}, f32[80,256]{1,0:T(8,128)}, u32[]{:S(2)}) copy-start(f32[80,256]{1,0:T(8,128)} %data.1) | copy-start | bytes 245764
  6.1 0.8 %copy-start.5 = (f32[32,256]{1,0:T(8,128)S(1)}, f32[32,256]{1,0:T(8,128)}, u32[]{:S(2)}) copy-start(f32[32,256]{1,0:T(8,128)} %coef.1) | copy-start | bytes 98308
  6.9 0.7 %copy-start.8 = (s32[32]{0:T(128)S(1)}, s32[32]{0:T(128)}, u32[]{:S(2)}) copy-start(s32[32]{0:T(128)} %lpar.1) | copy-start | bytes 388

commit v2 on v1

--- a/solution.py
+++ b/solution.py
@@ -26,25 +26,37 @@
     return contract(ah, bh, ca, cb) + (contract(ah, bl, ca, cb) + contract(al, bh, ca, cb))
 
 
+def flipped(index, bits, count):
+    out = index
+    place = 1
+    while place < count:
+        if bits & place:
+            out = out + place * (1 - 2 * lax.rem(lax.div(index, place), 2))
+        place *= 2
+    return out
+
+
 def kernel(
     groups, shards, capacity,
+    tgt_h, coef_h, data_h, lmap_h, lpar_h, inv_h, off_h, tinv_h, trhs_h,
+    leaf_out, top_out,
     tgt, coef, data, lmap, lpar, inv, off, tinv, trhs,
-    leaf_out, top_out,
-    send, recv, packed, wide, base, parts, arrived, tinv_v, trhs_v,
-    d_send, d_recv, f_send, f_recv, r_send, r_recv, g_send, g_recv, l_sem,
+    send, recv, packed, wide, base, parts, across, joined, along,
+    d_send, d_recv, f_send, f_recv, a_send, a_recv, z_send, z_recv, g_send, g_recv, l_sem,
 ):
     me = lax.axis_index("leaf")
     shard = lax.axis_index("rhs")
     local, width = inv.shape[0], inv.shape[1]
     coef_rows, rows = coef.shape
     dates = data.shape[0]
-    top_each = tinv_v.shape[0]
+    top_each = tinv.shape[0]
     total = lmap.shape[0]
     fold = LANES // coef_rows
     piece = capacity // fold
     pair = f_send.shape[1]
     per = groups // pair
-    leaf_peers = [lax.rem(me + o, groups) for o in range(groups)]
+    leaf_peers = [flipped(me, o, groups) for o in range(groups)]
+    far_first = sorted(range(1, groups), key=lambda o: (-(o.bit_length()), o))
     rhs_peers = [lax.rem(shard + o, shards) for o in range(shards)]
 
     barrier = pltpu.get_barrier_semaphore()
@@ -53,10 +65,25 @@
     for o in range(1, shards):
         pl.semaphore_signal(barrier, inc=1, device_id=(me, rhs_peers[o]), device_id_type=MESH)
     tops = pl.ds(me * top_each, top_each)
-    load_inv = pltpu.make_async_copy(tinv.at[tops], tinv_v, l_sem.at[0])
-    load_rhs = pltpu.make_async_copy(trhs.at[tops], trhs_v, l_sem.at[1])
-    load_inv.start()
-    load_rhs.start()
+    loads = []
+    for i, (src, dst) in enumerate(
+        [
+            (tgt_h, tgt),
+            (lmap_h, lmap),
+            (coef_h, coef),
+            (data_h, data),
+            (lpar_h, lpar),
+            (inv_h, inv),
+            (off_h, off),
+            (tinv_h.at[tops], tinv),
+            (trhs_h.at[tops], trhs),
+        ]
+    ):
+        copy = pltpu.make_async_copy(src, dst, l_sem.at[i])
+        copy.start()
+        loads.append(copy)
+    loads[0].wait()
+    loads[1].wait()
 
     target = tgt[...]
     position = jnp.zeros_like(target)
@@ -77,6 +104,8 @@
     chosen = jnp.concatenate(
         [jnp.where(slot_ids == slot[d : d + 1, :], 1.0, 0.0) for d in range(groups)], axis=0
     ).astype(BF16)
+    loads[2].wait()
+    loads[3].wait()
     fields = jnp.concatenate(
         [
             coef[...],
@@ -90,8 +119,8 @@
     send[...] = payload.reshape(groups, capacity, LANES)
 
     pl.semaphore_wait(barrier, groups - 1 + shards - 1)
-    row_copies = []
-    for o in range(1, groups):
+    row_copies = {}
+    for o in far_first:
         copy = pltpu.make_async_remote_copy(
             src_ref=send.at[leaf_peers[o]],
             dst_ref=recv.at[o],
@@ -101,18 +130,18 @@
             device_id_type=MESH,
         )
         copy.start()
-        row_copies.append(copy)
+        row_copies[o] = copy
     recv[0] = send[me]
 
+    for copy in loads[4:]:
+        copy.wait()
     for l in range(local):
         high, low = split(dot3(split(off[l]), split(inv[l]), 1, 0))
         wide[0, l] = high
         wide[1, l] = low
-    load_inv.wait()
-    load_rhs.wait()
     gram = []
     for i in range(top_each):
-        block = split(tinv_v[i])
+        block = split(tinv[i])
         gram.append(split(dot3(block, block, 0, 0)))
     up = []
     for l in range(local):
@@ -126,7 +155,7 @@
     for g in range(pair):
         for o in range(g * per, (g + 1) * per):
             if o > 0:
-                row_copies[o - 1].wait_recv()
+                row_copies[o].wait_recv()
             block = recv[o]
             out = block[:piece]
             for q in range(1, fold):
@@ -176,48 +205,80 @@
             term = jnp.where(up[l] == p, 1.0, 0.0) * updates[l]
             acc = term if acc is None else acc + term
         parts[p] = acc
-    sums = []
-    for o in range(1, groups):
+    steps = [h // 2 for h in far_first if h % 2 == 0] + [0]
+    cross = {}
+    for h in steps:
         copy = pltpu.make_async_remote_copy(
-            src_ref=parts.at[pl.ds(leaf_peers[o] * top_each, top_each)],
-            dst_ref=arrived.at[o],
-            send_sem=r_send.at[o],
-            recv_sem=r_recv.at[o],
-            device_id=(leaf_peers[o], shard),
+            src_ref=parts.at[pl.ds(leaf_peers[2 * h + 1] * top_each, top_each)],
+            dst_ref=across.at[h],
+            send_sem=a_send.at[h],
+            recv_sem=a_recv.at[h],
+            device_id=(leaf_peers[1], shard),
             device_id_type=MESH,
         )
         copy.start()
-        sums.append(copy)
+        cross[h] = copy
+    sums = {}
+    for h in steps:
+        cross[h].wait_recv()
+        here = parts[pl.ds(leaf_peers[2 * h] * top_each, top_each)] + across[h]
+        if h == 0:
+            residue = trhs[...] - here
+            continue
+        joined[h] = here
+        copy = pltpu.make_async_remote_copy(
+            src_ref=joined.at[h],
+            dst_ref=along.at[h],
+            send_sem=z_send.at[h],
+            recv_sem=z_recv.at[h],
+            device_id=(leaf_peers[2 * h], shard),
+            device_id_type=MESH,
+        )
+        copy.start()
+        sums[h] = copy
     for l in range(local):
         factor = split(inv[l])
         solved = split(dot3(rhs[l], factor, 1, 1))
         base[l] = dot3(solved, factor, 1, 0)
-    residue = [trhs_v[i] - parts[me * top_each + i] for i in range(top_each)]
-    for o in range(1, groups):
-        sums[o - 1].wait_recv()
-        residue = [residue[i] - arrived[o, i] for i in range(top_each)]
+    for h in steps[:-1]:
+        sums[h].wait_recv()
+        residue = residue - along[h]
     for i in range(top_each):
         top_out[me * top_each + i] = dot3(split(residue[i]), gram[i], 1, 0)
-    solutions = []
-    for o in range(1, groups):
+    solutions = {}
+    for o in steps[:-1]:
         copy = pltpu.make_async_remote_copy(
             src_ref=top_out.at[tops],
             dst_ref=top_out.at[tops],
-            send_sem=g_send.at[o],
-            recv_sem=g_recv.at[o],
-            device_id=(leaf_peers[o], shard),
+            send_sem=g_send.at[2 * o],
+            recv_sem=g_recv.at[2 * o],
+            device_id=(leaf_peers[2 * o], shard),
             device_id_type=MESH,
         )
         copy.start()
-        solutions.append(copy)
-    for copy in row_copies + forwards + sums:
+        solutions[2 * o] = copy
+    for h in reversed(steps):
+        if h > 0:
+            solutions[2 * h].wait_recv()
+        block = pl.ds(leaf_peers[2 * h] * top_each, top_each)
+        copy = pltpu.make_async_remote_copy(
+            src_ref=top_out.at[block],
+            dst_ref=top_out.at[block],
+            send_sem=g_send.at[2 * h + 1],
+            recv_sem=g_recv.at[2 * h + 1],
+            device_id=(leaf_peers[1], shard),
+            device_id_type=MESH,
+        )
+        copy.start()
+        solutions[2 * h + 1] = copy
+    for copy in [*row_copies.values(), *forwards, *cross.values(), *sums.values()]:
         copy.wait_send()
-    for copy in solutions:
-        copy.wait_recv()
+    for h in reversed(steps):
+        solutions[2 * h + 1].wait_recv()
     for l in range(local):
         lifted = dot3(split(top_out[up[l]]), (wide[0, l], wide[1, l]), 1, 0)
         leaf_out[l] = base[l] - lifted
-    for copy in solutions:
+    for copy in solutions.values():
         copy.wait_send()
 
 
@@ -232,10 +293,9 @@
     top_each = top_count // groups
     coef_rows = obs_coef.shape[0]
     piece = capacity * coef_rows // LANES
-    pair = groups // 2 if groups % 2 == 0 else groups
+    pair = groups // 2
     dma = pltpu.SemaphoreType.DMA
     vmem = pl.BlockSpec(memory_space=pltpu.VMEM)
-    smem = pl.BlockSpec(memory_space=pltpu.SMEM)
     hbm = pl.BlockSpec(memory_space=pl.ANY)
     return pl.pallas_call(
         functools.partial(kernel, groups, shards, capacity),
@@ -243,30 +303,41 @@
             jax.ShapeDtypeStruct((local, dates, width), F32),
             jax.ShapeDtypeStruct((top_count, dates, width), F32),
         ),
-        in_specs=[vmem, vmem, vmem, smem, smem, vmem, vmem, hbm, hbm],
+        in_specs=[hbm] * 9,
         out_specs=(vmem, vmem),
         scratch_shapes=[
+            pltpu.VMEM((1, rows), jnp.int32),
+            pltpu.VMEM(obs_coef.shape, F32),
+            pltpu.VMEM(obs_data.shape, F32),
+            pltpu.SMEM(leaf_map.shape, jnp.int32),
+            pltpu.SMEM(leaf_parent.shape, jnp.int32),
+            pltpu.VMEM(leaf_inv.shape, F32),
+            pltpu.VMEM(leaf_off.shape, F32),
+            pltpu.VMEM((top_each, width, width), F32),
+            pltpu.VMEM((top_each, dates, width), F32),
             pltpu.VMEM((groups, capacity, LANES), F32),
             pltpu.VMEM((groups, capacity, LANES), F32),
             pltpu.VMEM((shards, groups, piece, LANES), F32),
             pltpu.VMEM((2, local, width, width), BF16),
             pltpu.VMEM((local, dates, width), F32),
             pltpu.VMEM((top_count, dates, width), F32),
-            pltpu.VMEM((groups, top_each, dates, width), F32),
-            pltpu.VMEM((top_each, width, width), F32),
-            pltpu.VMEM((top_each, dates, width), F32),
+            pltpu.VMEM((groups // 2, top_each, dates, width), F32),
+            pltpu.VMEM((groups // 2, top_each, dates, width), F32),
+            pltpu.VMEM((groups // 2, top_each, dates, width), F32),
             dma((groups,)),
             dma((groups,)),
             dma((shards, pair)),
             dma((shards, pair)),
+            dma((groups // 2,)),
+            dma((groups // 2,)),
+            dma((groups // 2,)),
+            dma((groups // 2,)),
             dma((groups,)),
             dma((groups,)),
-            dma((groups,)),
-            dma((groups,)),
-            dma((2,)),
+            dma((9,)),
         ],
         compiler_params=pltpu.CompilerParams(
-            collective_id=0, has_side_effects=True, vmem_limit_bytes=24 * 2**20
+            collective_id=0, has_side_effects=True, vmem_limit_bytes=60 * 2**20
         ),
     )(
         obs_target.reshape(1, rows), obs_coef, obs_data, leaf_map, leaf_parent,
@@ -340,6 +411,8 @@
     dates = obs_data.shape[0]
     fits = (
         args[7].shape[0] % groups == 0
+        and groups > 1
+        and groups & (groups - 1) == 0
         and rows % LANES == 0
         and (2 * rows) % groups == 0
         and LANES % coef_rows == 0

time: 43.6 us -> 38.4 us (0.88)
  local copies, waits for them, and re-layouts: 8.28 us -> 2.37 us
  Pallas kernels: 34.2 us -> 35.3 us
    unnamed x20 -> x4, local copies, waits for them, and re-layouts: 8.28 us -> 2.37 us
    pallas_call x1, Pallas kernels: 34.2 us -> 35.3 us  [fused(): pl.pallas_call(functools.partial(kernel, groups, shards, capacity), out_s...]
where the time goes in v2:
time: 38.4 us; the launch traced here: 38.3 us
  Pallas kernels  35.3 us (92%)
  local copies, waits for them, and re-layouts  2.37 us (6%)
  between operations  0.65 us (2%)
    pallas_call x1, Pallas kernels, fused(): pl.pallas_call(functools.partial(kernel, groups, shards, capacity), out_s...  35.3 us
    unnamed x4, local copies, waits for them, and re-layouts  2.37 us

profile of v2, /device:TPU:0, one launch (start us, length us, event | category | flops | bytes accessed | tf_op | source)
XLA Modules:
  0.0 38.3 jit_solution(9925975758564689845)
XLA Ops:
  0.6 35.3 %shard_map.104 = (f32[4,80,128]{2,1,0:T(8,128)}, f32[8,80,128]{2,1,0:T(8,128)}) custom-call(s32[1,256]{1,0:T(1,128)} %bitcast.1, f32[32,256]{1,0:T(8,128)} %coef_h.1, f32[80,256]{1,0:T(8,128)} %data_h.1, s32[32]{0:T(128)} %lmap_h.1, s32[32]{0:T(128)} %lpar_h.1, f32[4,128,128]{2,1,0:T(8,128)} %inv_h.1, f32[4,128,128]{2,1,0:T(8,128)} %off_h.1, ...), custom_call_target="tpu_custom_call" | custom-call | tf_op jit(solution)/shard_map/pallas_call | solution.py:300
  35.9 0.0 copy-start
  35.9 1.6 %copy.13 = f32[4,80,128]{2,1,0:T(8,128)} copy(f32[4,80,128]{2,1,0:T(8,128)} %get-tuple-element.4) | data formatting | bytes 327680
  37.6 0.0 copy-done
  37.6 0.7 %copy.14 = f32[8,80,128]{2,1,0:T(8,128)} copy(f32[8,80,128]{2,1,0:T(8,128)S(1)} %copy-done) | data formatting | bytes 655360
Async XLA Ops:
  35.9 1.7 %copy-start = (f32[8,80,128]{2,1,0:T(8,128)S(1)}, f32[8,80,128]{2,1,0:T(8,128)}, u32[]{:S(2)}) copy-start(f32[8,80,128]{2,1,0:T(8,128)} %get-tuple-element.5) | copy-start | bytes 983044

commit v3 on v2

--- a/solution.py
+++ b/solution.py
@@ -54,6 +54,7 @@
     fold = LANES // coef_rows
     piece = capacity // fold
     pair = f_send.shape[1]
+    cuts, tops_all, half = parts.shape[0], parts.shape[1], parts.shape[2]
     per = groups // pair
     leaf_peers = [flipped(me, o, groups) for o in range(groups)]
     far_first = sorted(range(1, groups), key=lambda o: (-(o.bit_length()), o))
@@ -89,7 +90,10 @@
     position = jnp.zeros_like(target)
     for i in range(total):
         position = jnp.where(target == i, lmap[i], position)
-    first = lax.broadcasted_iota(jnp.int32, (groups, rows), 0) * local
+    place = lax.broadcasted_iota(jnp.int32, (groups, rows), 0)
+    first = jnp.zeros_like(place)
+    for o in range(groups):
+        first = jnp.where(place == o, leaf_peers[o] * local, first)
     member = jnp.broadcast_to(position, (groups, rows)) - first
     owned = (member >= 0) & (member < local)
     hot = jnp.where(owned, 1.0, 0.0)
@@ -101,9 +105,6 @@
     slot = jnp.where(owned, rank.astype(jnp.int32), -1)
     mark = jnp.sum(hot * (member + 1).astype(F32), axis=0, keepdims=True)
     slot_ids = lax.broadcasted_iota(jnp.int32, (capacity, rows), 0)
-    chosen = jnp.concatenate(
-        [jnp.where(slot_ids == slot[d : d + 1, :], 1.0, 0.0) for d in range(groups)], axis=0
-    ).astype(BF16)
     loads[2].wait()
     loads[3].wait()
     fields = jnp.concatenate(
@@ -115,14 +116,17 @@
         axis=0,
     )
     high, low = split(fields)
-    payload = contract(chosen, high, 1, 1) + contract(chosen, low, 1, 1)
-    send[...] = payload.reshape(groups, capacity, LANES)
+
+    def placed(o):
+        chosen = jnp.where(slot_ids == slot[o : o + 1, :], 1.0, 0.0).astype(BF16)
+        return contract(chosen, high, 1, 1) + contract(chosen, low, 1, 1)
 
     pl.semaphore_wait(barrier, groups - 1 + shards - 1)
     row_copies = {}
     for o in far_first:
+        send[o] = placed(o)
         copy = pltpu.make_async_remote_copy(
-            src_ref=send.at[leaf_peers[o]],
+            src_ref=send.at[o],
             dst_ref=recv.at[o],
             send_sem=d_send.at[o],
             recv_sem=d_recv.at[o],
@@ -131,7 +135,7 @@
         )
         copy.start()
         row_copies[o] = copy
-    recv[0] = send[me]
+    recv[0] = placed(0)
 
     for copy in loads[4:]:
         copy.wait()
@@ -196,88 +200,97 @@
         [jnp.where(marks == float(l + 1), coefs, 0.0) for l in range(local)], axis=1
     )
     rhs_all = dot3(turned, split(spread), 1, 0)[coef_rows : coef_rows + dates]
-    rhs = [split(rhs_all[:, l * width : (l + 1) * width]) for l in range(local)]
-    updates = [dot3(rhs[l], (wide[0, l], wide[1, l]), 1, 1) for l in range(local)]
-    tops_all = top_out.shape[0]
-    for p in range(tops_all):
-        acc = None
-        for l in range(local):
-            term = jnp.where(up[l] == p, 1.0, 0.0) * updates[l]
-            acc = term if acc is None else acc + term
-        parts[p] = acc
+    rhs = [
+        [split(rhs_all[n : n + half, l * width : (l + 1) * width]) for l in range(local)]
+        for n in range(0, dates, half)
+    ]
     steps = [h // 2 for h in far_first if h % 2 == 0] + [0]
-    cross = {}
-    for h in steps:
+    cross, sums, solutions = {}, {}, {}
+    weight = [[jnp.where(up[l] == p, 1.0, 0.0) for p in range(tops_all)] for l in range(local)]
+    for n in range(cuts):
+        updates = [dot3(rhs[n][l], (wide[0, l], wide[1, l]), 1, 1) for l in range(local)]
+        for p in range(tops_all):
+            acc = weight[0][p] * updates[0]
+            for l in range(1, local):
+                acc = acc + weight[l][p] * updates[l]
+            parts[n, p] = acc
+        for h in steps:
+            copy = pltpu.make_async_remote_copy(
+                src_ref=parts.at[n, pl.ds(leaf_peers[2 * h + 1] * top_each, top_each)],
+                dst_ref=across.at[n, h],
+                send_sem=a_send.at[n, h],
+                recv_sem=a_recv.at[n, h],
+                device_id=(leaf_peers[1], shard),
+                device_id_type=MESH,
+            )
+            copy.start()
+            cross[n, h] = copy
+    residue = []
+    for n in range(cuts):
+        for h in steps:
+            cross[n, h].wait_recv()
+            here = parts[n, pl.ds(leaf_peers[2 * h] * top_each, top_each)] + across[n, h]
+            if h == 0:
+                residue.append(trhs[:, n * half : (n + 1) * half] - here)
+                continue
+            joined[n, h] = here
+            copy = pltpu.make_async_remote_copy(
+                src_ref=joined.at[n, h],
+                dst_ref=along.at[n, h],
+                send_sem=z_send.at[n, h],
+                recv_sem=z_recv.at[n, h],
+                device_id=(leaf_peers[2 * h], shard),
+                device_id_type=MESH,
+            )
+            copy.start()
+            sums[n, h] = copy
+    for l in range(local):
+        factor = split(inv[l])
+        for n in range(cuts):
+            solved = split(dot3(rhs[n][l], factor, 1, 1))
+            base[l, n * half : (n + 1) * half] = dot3(solved, factor, 1, 0)
+
+    def pass_on(n, h, o, peer):
+        block = top_out.at[pl.ds(leaf_peers[h] * top_each, top_each), pl.ds(n * half, half)]
         copy = pltpu.make_async_remote_copy(
-            src_ref=parts.at[pl.ds(leaf_peers[2 * h + 1] * top_each, top_each)],
-            dst_ref=across.at[h],
-            send_sem=a_send.at[h],
-            recv_sem=a_recv.at[h],
-            device_id=(leaf_peers[1], shard),
+            src_ref=block,
+            dst_ref=block,
+            send_sem=g_send.at[n, o],
+            recv_sem=g_recv.at[n, o],
+            device_id=(leaf_peers[peer], shard),
             device_id_type=MESH,
         )
         copy.start()
-        cross[h] = copy
-    sums = {}
-    for h in steps:
-        cross[h].wait_recv()
-        here = parts[pl.ds(leaf_peers[2 * h] * top_each, top_each)] + across[h]
-        if h == 0:
-            residue = trhs[...] - here
-            continue
-        joined[h] = here
-        copy = pltpu.make_async_remote_copy(
-            src_ref=joined.at[h],
-            dst_ref=along.at[h],
-            send_sem=z_send.at[h],
-            recv_sem=z_recv.at[h],
-            device_id=(leaf_peers[2 * h], shard),
-            device_id_type=MESH,
-        )
-        copy.start()
-        sums[h] = copy
-    for l in range(local):
-        factor = split(inv[l])
-        solved = split(dot3(rhs[l], factor, 1, 1))
-        base[l] = dot3(solved, factor, 1, 0)
-    for h in steps[:-1]:
-        sums[h].wait_recv()
-        residue = residue - along[h]
-    for i in range(top_each):
-        top_out[me * top_each + i] = dot3(split(residue[i]), gram[i], 1, 0)
-    solutions = {}
-    for o in steps[:-1]:
-        copy = pltpu.make_async_remote_copy(
-            src_ref=top_out.at[tops],
-            dst_ref=top_out.at[tops],
-            send_sem=g_send.at[2 * o],
-            recv_sem=g_recv.at[2 * o],
-            device_id=(leaf_peers[2 * o], shard),
-            device_id_type=MESH,
-        )
-        copy.start()
-        solutions[2 * o] = copy
-    for h in reversed(steps):
-        if h > 0:
-            solutions[2 * h].wait_recv()
-        block = pl.ds(leaf_peers[2 * h] * top_each, top_each)
-        copy = pltpu.make_async_remote_copy(
-            src_ref=top_out.at[block],
-            dst_ref=top_out.at[block],
-            send_sem=g_send.at[2 * h + 1],
-            recv_sem=g_recv.at[2 * h + 1],
-            device_id=(leaf_peers[1], shard),
-            device_id_type=MESH,
-        )
-        copy.start()
-        solutions[2 * h + 1] = copy
+        solutions[n, o] = copy
+
+    for n in range(cuts):
+        left = residue[n]
+        for h in steps[:-1]:
+            sums[n, h].wait_recv()
+            left = left - along[n, h]
+        for i in range(top_each):
+            top_out[me * top_each + i, n * half : (n + 1) * half] = dot3(
+                split(left[i]), gram[i], 1, 0
+            )
+        for h in steps[:-1]:
+            pass_on(n, 0, 2 * h, 2 * h)
+        pass_on(n, 0, 1, 1)
+    for n in range(cuts):
+        for h in reversed(steps[:-1]):
+            solutions[n, 2 * h].wait_recv()
+            pass_on(n, 2 * h, 2 * h + 1, 1)
     for copy in [*row_copies.values(), *forwards, *cross.values(), *sums.values()]:
         copy.wait_send()
-    for h in reversed(steps):
-        solutions[2 * h + 1].wait_recv()
-    for l in range(local):
-        lifted = dot3(split(top_out[up[l]]), (wide[0, l], wide[1, l]), 1, 0)
-        leaf_out[l] = base[l] - lifted
+    for n in range(cuts):
+        for h in reversed(steps):
+            solutions[n, 2 * h + 1].wait_recv()
+        dates_here = slice(n * half, (n + 1) * half)
+        for l in range(local):
+            own = weight[l][0] * top_out[0, dates_here]
+            for p in range(1, tops_all):
+                own = own + weight[l][p] * top_out[p, dates_here]
+            lifted = dot3(split(own), (wide[0, l], wide[1, l]), 1, 0)
+            leaf_out[l, dates_here] = base[l, dates_here] - lifted
     for copy in solutions.values():
         copy.wait_send()
 
@@ -294,9 +307,11 @@
     coef_rows = obs_coef.shape[0]
     piece = capacity * coef_rows // LANES
     pair = groups // 2
+    cuts = 2 if dates % 16 == 0 else 1
+    half = dates // cuts
     dma = pltpu.SemaphoreType.DMA
     vmem = pl.BlockSpec(memory_space=pltpu.VMEM)
-    hbm = pl.BlockSpec(memory_space=pl.ANY)
+    hbm = pl.BlockSpec(memory_space=pltpu.HBM)
     return pl.pallas_call(
         functools.partial(kernel, groups, shards, capacity),
         out_shape=(
@@ -320,28 +335,33 @@
             pltpu.VMEM((shards, groups, piece, LANES), F32),
             pltpu.VMEM((2, local, width, width), BF16),
             pltpu.VMEM((local, dates, width), F32),
-            pltpu.VMEM((top_count, dates, width), F32),
-            pltpu.VMEM((groups // 2, top_each, dates, width), F32),
-            pltpu.VMEM((groups // 2, top_each, dates, width), F32),
-            pltpu.VMEM((groups // 2, top_each, dates, width), F32),
+            pltpu.VMEM((cuts, top_count, half, width), F32),
+            pltpu.VMEM((cuts, groups // 2, top_each, half, width), F32),
+            pltpu.VMEM((cuts, groups // 2, top_each, half, width), F32),
+            pltpu.VMEM((cuts, groups // 2, top_each, half, width), F32),
             dma((groups,)),
             dma((groups,)),
             dma((shards, pair)),
             dma((shards, pair)),
-            dma((groups // 2,)),
-            dma((groups // 2,)),
-            dma((groups // 2,)),
-            dma((groups // 2,)),
-            dma((groups,)),
-            dma((groups,)),
+            dma((cuts, groups // 2)),
+            dma((cuts, groups // 2)),
+            dma((cuts, groups // 2)),
+            dma((cuts, groups // 2)),
+            dma((cuts, groups)),
+            dma((cuts, groups)),
             dma((9,)),
         ],
         compiler_params=pltpu.CompilerParams(
-            collective_id=0, has_side_effects=True, vmem_limit_bytes=60 * 2**20
+            collective_id=0, has_side_effects=True, vmem_limit_bytes=24 * 2**20
         ),
     )(
-        obs_target.reshape(1, rows), obs_coef, obs_data, leaf_map, leaf_parent,
-        leaf_inv, leaf_off, top_inv, top_rhs,
+        *(
+            pltpu.with_memory_space_constraint(x, pltpu.HBM)
+            for x in (
+                obs_target.reshape(1, rows), obs_coef, obs_data, leaf_map, leaf_parent,
+                leaf_inv, leaf_off, top_inv, top_rhs,
+            )
+        )
     )
 
 

time: 38.4 us -> 36.5 us (0.951)
  local copies, waits for them, and re-layouts: 2.37 us -> 1.39 us
  Pallas kernels: 35.3 us -> 34.4 us
    unnamed x4 -> x2, local copies, waits for them, and re-layouts: 2.37 us -> 1.39 us
    pallas_call x1, Pallas kernels: 35.3 us -> 34.4 us  [fused(): pl.pallas_call(functools.partial(kernel, groups, shards, capacity), out_s...]
where the time goes in v3:
time: 36.5 us; the launch traced here: 36.4 us
  Pallas kernels  34.4 us (94%)
  local copies, waits for them, and re-layouts  1.39 us (4%)
  between operations  0.64 us (2%)
    pallas_call x1, Pallas kernels, fused(): pl.pallas_call(functools.partial(kernel, groups, shards, capacity), out_s...  34.4 us
    unnamed x2, local copies, waits for them, and re-layouts  1.39 us

profile of v3, /device:TPU:0, one launch (start us, length us, event | category | flops | bytes accessed | tf_op | source)
XLA Modules:
  0.0 36.4 jit_solution(3465683450446304732)
XLA Ops:
  0.6 34.4 %shard_map.104 = (f32[4,80,128]{2,1,0:T(8,128)S(1)}, f32[8,80,128]{2,1,0:T(8,128)S(1)}) custom-call(s32[1,256]{1,0:T(1,128)} %bitcast.1, f32[32,256]{1,0:T(8,128)} %coef_h.1, f32[80,256]{1,0:T(8,128)} %data_h.1, s32[32]{0:T(128)} %lmap_h.1, s32[32]{0:T(128)} %lpar_h.1, f32[4,128,128]{2,1,0:T(8,128)} %inv_h.1, f32[4,128,128]{2,1,0:T(8,128)} %off_h.1, ...), custom_call_target="tpu_custom_call" | custom-call | tf_op jit(solution)/shard_map/pallas_call | solution.py:315
  35.0 0.7 %copy.13 = f32[4,80,128]{2,1,0:T(8,128)} copy(f32[4,80,128]{2,1,0:T(8,128)S(1)} %get-tuple-element.4) | data formatting | bytes 327680
  35.7 0.7 %copy.14 = f32[8,80,128]{2,1,0:T(8,128)} copy(f32[8,80,128]{2,1,0:T(8,128)S(1)} %get-tuple-element.5) | data formatting | bytes 655360
